TPU v7x, 256 devices: a whole 4x4x8 slice. The times are simulated.
256 devices in a mesh: replica: 16 (over y, z_lo), fsdp: 16 (over x, z_hi, core).
Axes of the slice: x: 4, y: 4, z: 8 (z_hi: 2, z_lo: 4; z = z_hi * 4 + z_lo), core: 2. Of those that a mesh axis runs over, the one named last changes fastest.
Arguments:
- local_weights: float32 [16, 5120, 512], P('replica', 'fsdp')
- outer_base: float32 [5120, 512], P('fsdp')
- outer_momentum: float32 [5120, 512], P(('fsdp', 'replica')), may hold values from -4 to 4
- batch: bfloat16 [16, 2, 6144, 5120], P('replica', None, 'fsdp'), may hold values from -6 to 6
- cotangent: bfloat16 [16, 2, 6144, 512], P('replica', None, 'fsdp'), may hold values from -6 to 6
- step: int32 [1], replicated, may hold values from 0 to 4095
- plan: int32 [8], replicated, may hold values from 0 to 3
Outputs:
- new_weights: float32 [16, 5120, 512], P('replica', 'fsdp')
- new_base: float32 [5120, 512], P('fsdp')
- new_momentum: float32 [5120, 512], P(('fsdp', 'replica'))
All inputs are finite; a program needn't handle non-finite values. Where the computation divides by a largest or mean magnitude, that divisor is 1e-20 or more.
Results may differ from a plain program's by a relative error of at most 0.0055.
Values may be sent and summed in bfloat16 or wider, within the bound.
No kernel may reach another device: no remote copies, remote signals or barrier semaphores. Data moves between devices by JAX's collectives and lax.ppermute only.
A program may use at most 128 MiB of HBM per device.

v0:
```python
import jax
import jax.numpy as jnp
from jax import lax
from jax.sharding import PartitionSpec as P

D = 5120
HEAD_DIM = 128
SCHED_LEN = 8
INNER = 2
eps_norm = 1e-06
eps_scale = 1e-06
inner_rate = 0.5
outer_rate = 0.7
outer_decay = 0.9
mix_local = 0.5


def pick_fragment(step, plan):
    position = step[0] % SCHED_LEN
    hits = jnp.arange(SCHED_LEN, dtype=jnp.int32) == position
    return jnp.sum(jnp.where(hits, plan, 0))


def rate_of(step):
    return outer_rate * 1024.0 / (1024.0 + step[0].astype(jnp.float32))


def normalize(rows):
    values = rows.astype(jnp.float32)
    mean_square = jnp.mean(values * values, axis=-1, keepdims=True)
    return (values * lax.rsqrt(mean_square + eps_norm)).astype(jnp.bfloat16)


def silu_slope(values):
    gate_value = jax.nn.sigmoid(values)
    return gate_value * (1.0 + values * (1.0 - gate_value))


def on_device(local_weights, outer_base, outer_momentum, batch, cotangent, step, plan):
    inv_width = D ** (-0.5)
    fragment = pick_fragment(step, plan)
    outer_lr = rate_of(step)
    first_col = fragment * HEAD_DIM
    weights = local_weights[0]
    base_cols = lax.dynamic_slice_in_dim(outer_base, first_col, HEAD_DIM, 1)
    pseudo_grad = base_cols - lax.dynamic_slice_in_dim(weights, first_col, HEAD_DIM, 1)
    block_scale = (jnp.max(jnp.abs(pseudo_grad), axis=1) + eps_scale).astype(jnp.bfloat16)
    codes_out = (pseudo_grad / block_scale.astype(jnp.float32)[:, None]).astype(jnp.bfloat16)
    moment_cols = lax.dynamic_slice_in_dim(outer_momentum, first_col, HEAD_DIM, 1)
    share_rows = moment_cols.shape[0]
    share_first = lax.axis_index("replica") * share_rows
    replicas = lax.axis_size("replica")
    dequant = (
        lax.all_gather(codes_out[None], "replica", axis=0, tiled=True).astype(jnp.float32)
        * lax.all_gather(block_scale[None], "replica", axis=0, tiled=True).astype(jnp.float32)[
            :, :, None
        ]
    )
    running = jnp.sum(dequant, axis=0)
    average = running / replicas
    moment_all = lax.all_gather(moment_cols, "replica", axis=0, tiled=True)
    moment_full = outer_decay * moment_all + average
    base_frag = base_cols - outer_lr * (outer_decay * moment_full + average)
    moment_new = lax.dynamic_slice_in_dim(moment_full, share_first, share_rows, 0)
    for index in range(INNER):
        normed = normalize(batch[0, index])
        cot_rows = cotangent[0, index].astype(jnp.float32)
        values = (
            jnp.dot(
                normed,
                lax.all_gather(weights.astype(jnp.bfloat16), "fsdp", axis=0, tiled=True),
                preferred_element_type=jnp.float32,
            )
            * inv_width
        )
        slopes = (cot_rows * silu_slope(values)).astype(jnp.bfloat16)
        gradient = lax.psum_scatter(
            jnp.dot(normed.T, slopes, preferred_element_type=jnp.float32).astype(jnp.bfloat16),
            "fsdp",
            scatter_dimension=0,
            tiled=True,
        ).astype(jnp.float32)
        weights = weights - inner_rate * inv_width * gradient
    trained_cols = lax.dynamic_slice_in_dim(weights, first_col, HEAD_DIM, 1)
    blended = mix_local * trained_cols + (1.0 - mix_local) * base_frag
    new_weights = lax.dynamic_update_slice_in_dim(weights, blended, first_col, 1)[None]
    new_base = lax.dynamic_update_slice_in_dim(outer_base, base_frag, first_col, 1)
    new_momentum = lax.dynamic_update_slice_in_dim(outer_momentum, moment_new, first_col, 1)
    return (new_weights, new_base, new_momentum)


def solution(mesh):
    placed = (
        P("replica", "fsdp", None),
        P("fsdp", None),
        P(("fsdp", "replica"), None),
        P("replica", None, "fsdp", None),
        P("replica", None, "fsdp", None),
        P(),
        P(),
    )
    return jax.shard_map(
        on_device,
        mesh=mesh,
        in_specs=placed,
        out_specs=(P("replica", "fsdp", None), P("fsdp", None), P(("fsdp", "replica"), None)),
        check_vma=False,
    )
```

profile of v0, /device:TPU:8, one launch (start us, length us, event | category | flops | bytes accessed | tf_op | source)
XLA Modules:
  0.0 509.7 jit_solution(3439085764657868025)
XLA Ops:
  7.2 0.0 copy-start.5
  7.2 0.0 all-gather.7.cloned.1.call-start
  7.2 1.2 copy.17
  8.4 0.8 copy.18
  9.2 1.9 bitcast_convert_fusion
  11.0 0.0 all-gather.7.cloned.1.call-update
  11.0 0.0 reduce-scatter.3.cloned.1.call-start
  11.1 4.2 fusion
  15.3 83.7 %all-gather.7.cloned.1.call-done = bf16[5120,512]{1,0:T(8,128)(2,1)} async-done(((bf16[320,512]{1,0:T(8,128)(2,1)}), bf16[5120,512]{1,0:T(8,128)(2,1)}) %all-gather.7.cloned.1.call-update) | async-done | bytes 5242896 | tf_op jit(solution)/shard_map/all_gather | solution.py:71
  99.0 0.0 copy-done.5
  99.0 12.4 %convolution_convert_fusion.1 = bf16[5120,512]{1,0:T(8,128)(2,1)} fusion(f32[384]{0:T(512)S(1)} %add_rsqrt_fusion.1, bf16[1,2,384,5120]{3,2,1,0:T(8,128)(2,1)} %param.10, bf16[5120,512]{1,0:T(8,128)(2,1)} %all-gather.7.cloned.1.call-done, bf16[1,2,384,512]{3,2,1,0:T(8,128)(2,1)S(1)} %copy-done.5), kind=kOutput, calls=%fused_computation.9 | convolution fusion | flops 4043112448 | bytes 18747392 | tf_op jit(solution)/shard_map/dot_general | solution.py:78
  111.4 0.0 copy-start
  111.4 0.0 copy-start.6
  111.4 0.0 reduce-scatter.3.cloned.1.call-update
  111.4 0.0 all-gather.9.cloned.1.call-start
  111.5 107.9 %reduce-scatter.3.cloned.1.call-done = bf16[320,512]{1,0:T(8,128)(2,1)} async-done(((bf16[5120,512]{1,0:T(8,128)(2,1)}), bf16[320,512]{1,0:T(8,128)(2,1)}) %reduce-scatter.3.cloned.1.call-update) | async-done | bytes 327696 | tf_op jit(solution)/shard_map/reduce_scatter | solution.py:77
  219.3 0.0 copy-done
  219.3 1.8 fusion.19
  221.1 0.0 all-gather.9.cloned.1.call-update
  221.2 0.0 all-gather.11.cloned.1.call-start
  221.9 0.0 copy-done.6
  221.9 0.6 fusion.28
  223.2 0.2 abs_reduce_fusion
  223.3 0.8 divide_convert_fusion
  224.1 0.0 all-gather.11.cloned.1.call-update
  224.1 0.0 reduce-scatter.5.cloned.1.call-start
  224.2 79.1 %all-gather.9.cloned.1.call-done = bf16[5120,512]{1,0:T(8,128)(2,1)} async-done(((bf16[320,512]{1,0:T(8,128)(2,1)}), bf16[5120,512]{1,0:T(8,128)(2,1)}) %all-gather.9.cloned.1.call-update) | async-done | bytes 5242896 | tf_op jit(solution)/shard_map/all_gather | solution.py:71
  303.3 12.4 %convolution_convert_fusion = bf16[5120,512]{1,0:T(8,128)(2,1)} fusion(f32[384]{0:T(512)S(1)} %add_rsqrt_fusion, bf16[1,2,384,5120]{3,2,1,0:T(8,128)(2,1)} %param.10, bf16[5120,512]{1,0:T(8,128)(2,1)} %all-gather.9.cloned.1.call-done, bf16[1,2,384,512]{3,2,1,0:T(8,128)(2,1)S(1)} %copy-done.5), kind=kOutput, calls=%fused_computation.8 | convolution fusion | flops 4043112448 | bytes 18747392 | tf_op jit(solution)/shard_map/dot_general | solution.py:78
  315.7 0.0 copy-start.7
  315.7 0.0 copy-start.2
  315.7 0.0 reduce-scatter.5.cloned.1.call-update
  315.8 35.2 %all-gather.2 = f32[16,20,128]{2,1,0:T(8,128)S(1)} all-gather(f32[1,20,128]{2,1,0:T(8,128)S(1)} %dynamic-slice_bitcast_fusion), channel_id=1, replica_groups=mesh['replica'=16,'fsdp'=16] {'replica'}, dimensions={0}, use_global_device_ids=true | all-gather | bytes 174080 | tf_op jit(solution)/shard_map/all_gather | solution.py:61
  351.0 0.0 copy-done.7
  351.0 0.6 dynamic-slice.1
  352.3 0.3 dynamic-update-slice
  352.5 74.1 %all-reduce = bf16[5120]{0:T(1024)(128)(2,1)S(1)} all-reduce(bf16[5120]{0:T(1024)(128)(2,1)S(1)} %dynamic-update-slice), channel_id=3, replica_groups=mesh['replica'=16,'fsdp'=16] {'replica'}, use_global_device_ids=true, to_apply=%add | all-reduce | flops 5120 | bytes 20480
  426.6 0.1 reshape.59
  426.8 0.0 all-gather.11.cloned.1.call-done
  426.8 1.9 fusion.4
  428.7 72.1 %reduce-scatter.5.cloned.1.call-done = bf16[320,512]{1,0:T(8,128)(2,1)} async-done(((bf16[5120,512]{1,0:T(8,128)(2,1)}), bf16[320,512]{1,0:T(8,128)(2,1)}) %reduce-scatter.5.cloned.1.call-update) | async-done | bytes 327696 | tf_op jit(solution)/shard_map/reduce_scatter | solution.py:77
  500.8 0.0 copy-done.2
  500.8 1.1 multiply_subtract_fusion
  502.0 0.1 bitcast_dynamic-update-slice_fusion
  502.1 0.0 copy-start.3
  502.1 0.1 multiply_add_fusion
  502.2 0.0 copy-start.1
  502.2 0.0 copy-start.4
  502.2 0.7 copy-done.3
  502.9 0.2 copy-done.1
  503.1 0.0 copy-done.4
  (9 shorter events, 0.1 us)
Async XLA Ops:
  7.2 91.8 %copy-start.5 = (bf16[1,2,384,512]{3,2,1,0:T(8,128)(2,1)S(1)}, bf16[1,2,384,512]{3,2,1,0:T(8,128)(2,1)}, u32[]{:S(2)}) copy-start(bf16[1,2,384,512]{3,2,1,0:T(8,128)(2,1)} %param.11) | copy-start | bytes 2359300
  7.2 91.8 %all-gather.7.cloned.1.call-start = ((), (), s32[]{:S(2)}) async-start(), calls=%async_computation.2 | async-start | bytes 5570560 | tf_op jit(solution)/shard_map/all_gather | solution.py:71
  11.0 208.3 %reduce-scatter.3.cloned.1.call-start = ((), (), s32[]{:S(2)}) async-start(), calls=%async_computation.3 | async-start | bytes 5570560 | tf_op jit(solution)/shard_map/reduce_scatter | solution.py:77
  111.4 108.0 %copy-start = (f32[1,320,512]{2,1,0:T(8,128)S(1)}, f32[1,320,512]{2,1,0:T(8,128)}, u32[]{:S(2)}) copy-start(f32[1,320,512]{2,1,0:T(8,128)} %param.7) | copy-start | bytes 1966084
  111.4 110.5 %copy-start.6 = (s32[8]{0:T(128)S(1)}, s32[8]{0:T(128)}, u32[]{:S(2)}) copy-start(s32[8]{0:T(128)} %param.13) | copy-start | bytes 100
  111.4 191.9 %all-gather.9.cloned.1.call-start = ((), (), s32[]{:S(2)}) async-start(), calls=%async_computation.4 | async-start | bytes 5570560 | tf_op jit(solution)/shard_map/all_gather | solution.py:71
  221.2 205.6 %all-gather.11.cloned.1.call-start = ((), (), s32[]{:S(2)}) async-start(), calls=%async_computation.6 | async-start | bytes 1392640 | tf_op jit(solution)/shard_map/all_gather | solution.py:54
  224.1 276.7 %reduce-scatter.5.cloned.1.call-start = ((), (), s32[]{:S(2)}) async-start(), calls=%async_computation.5 | async-start | bytes 5570560 | tf_op jit(solution)/shard_map/reduce_scatter | solution.py:77
  315.7 35.3 %copy-start.7 = (u32[256]{0:T(256)S(1)}, u32[256]{0:T(256)}, u32[]{:S(2)}) copy-start(u32[256]{0:T(256)} %constant.63) | copy-start | bytes 3076
  315.7 185.1 %copy-start.2 = (bf16[320,512]{1,0:T(8,128)(2,1)S(1)}, bf16[320,512]{1,0:T(8,128)(2,1)}, u32[]{:S(2)}) copy-start(bf16[320,512]{1,0:T(8,128)(2,1)} %reduce-scatter.3.cloned.1.call-done) | copy-start | bytes 983044
  502.1 0.8 copy-start.3
  502.2 1.0 copy-start.1
  502.2 0.9 copy-start.4
Sparse Core Ops, SparseCore 0:
  11.3 87.6 all-gather.6
  111.5 107.7 reduce-scatter.2
  222.6 80.6 all-gather.8
  305.5 73.0 all-gather.10
  382.9 117.8 reduce-scatter.4
where the time goes:
time: 510 us
  waiting for transfers between devices  343 us (67%)
  blocking collectives  109 us (21%)
  matrix products  24.8 us (5%)
  between operations  16 us (3%)
  other arithmetic  12.6 us (2%)
    reduce_scatter x2, waiting for transfers between devices, on_device(): lax.psum_scatter(jnp.dot(normed.T, slopes, preferred_element_type=jnp.flo...  180 us
    all_gather x2, waiting for transfers between devices, on_device(): lax.all_gather(weights.astype(jnp.bfloat16), 'fsdp', axis=0, tiled=True)  163 us
    unnamed x1, blocking collectives  74.1 us
    all_gather x1, blocking collectives, on_device(): moment_all = lax.all_gather(moment_cols, 'replica', axis=0, tiled=True)  35.2 us
    dot_general x2, matrix products, on_device(): jnp.dot(normed.T, slopes, preferred_element_type=jnp.float32)  24.8 us
  transfers between devices with their start and end apart: 5, of which 4 were waited for; matrix products, arithmetic and copies ran while one was open for 4% of the time, Pallas kernels for 0%

commit v1 on v0

--- a/solution.py
+++ b/solution.py
@@ -68,7 +68,15 @@
         values = (
             jnp.dot(
                 normed,
-                lax.all_gather(weights.astype(jnp.bfloat16), "fsdp", axis=0, tiled=True),
+                jnp.concatenate(
+                    lax.all_to_all(
+                        jnp.stack([weights.astype(jnp.bfloat16)] * lax.axis_size("fsdp")),
+                        "fsdp",
+                        0,
+                        0,
+                    ),
+                    axis=0,
+                ),
                 preferred_element_type=jnp.float32,
             )
             * inv_width

time: 510 us -> 575 us (1.13); the launches traced: 510 us -> 567 us
  waiting for transfers between devices: 343 us -> 374 us
  starting transfers between devices: 0.21 us -> 16.1 us
    all_to_all x0 -> x2, waiting for transfers between devices: none -> 261 us  [on_device(): lax.all_to_all(jnp.stack([weights.astype(jnp.bfloat16)] * lax.axis_size('...]
    all_gather x2 -> x0, waiting for transfers between devices: 163 us -> none  [on_device(): lax.all_gather(weights.astype(jnp.bfloat16), 'fsdp', axis=0, tiled=True)]
    reduce_scatter x2, waiting for transfers between devices: 180 us -> 113 us  [on_device(): lax.psum_scatter(jnp.dot(normed.T, slopes, preferred_element_type=jnp.flo...]
    all_to_all x0 -> x2, starting transfers between devices: none -> 15.8 us  [on_device(): lax.all_to_all(jnp.stack([weights.astype(jnp.bfloat16)] * lax.axis_size('...]
  transfers between devices with their start and end apart: 5 -> 5, of which waited for: 4 -> 3; matrix products, arithmetic and copies ran while one was open for 4% -> 4% of each run, Pallas kernels for 0% -> 0%
where the time goes in v1:
time: 575 us; the launch traced here: 567 us
  waiting for transfers between devices  374 us (65%)
  blocking collectives  113 us (20%)
  matrix products  24.9 us (4%)
  between operations  17.7 us (3%)
  starting transfers between devices  16.1 us (3%)
  other arithmetic  11.2 us (2%)
  local copies, waits for them, and re-layouts  9.57 us (2%)
    all_to_all x2, waiting for transfers between devices, on_device(): lax.all_to_all(jnp.stack([weights.astype(jnp.bfloat16)] * lax.axis_size('...  261 us
    reduce_scatter x2, waiting for transfers between devices, on_device(): lax.psum_scatter(jnp.dot(normed.T, slopes, preferred_element_type=jnp.flo...  113 us
    unnamed x1, blocking collectives  78.4 us
    all_gather x1, blocking collectives, on_device(): moment_all = lax.all_gather(moment_cols, 'replica', axis=0, tiled=True)  34.9 us
    dot_general x2, matrix products, on_device(): jnp.dot(normed.T, slopes, preferred_element_type=jnp.float32)  24.9 us
    all_to_all x2, starting transfers between devices, on_device(): lax.all_to_all(jnp.stack([weights.astype(jnp.bfloat16)] * lax.axis_size('...  15.8 us
  transfers between devices with their start and end apart: 5, of which 3 were waited for; matrix products, arithmetic and copies ran while one was open for 4% of the time, Pallas kernels for 0%

profile of v1, /device:TPU:8, one launch (start us, length us, event | category | flops | bytes accessed | tf_op | source)
XLA Modules:
  0.0 566.8 jit_solution(10662509239985618815)
XLA Ops:
  8.0 1.1 copy.17
  9.1 0.8 copy.18
  9.9 1.1 convert_bitcast_fusion.2
  11.0 2.9 stack.7
  13.9 11.1 %all-to-all-start = ((bf16[16,320,512]{2,1,0:T(8,128)(2,1)}), bf16[16,320,512]{2,1,0:T(8,128)(2,1)}, u32[]{:S(2)}, u32[]{:S(2)}) async-start(bf16[16,320,512]{2,1,0:T(8,128)(2,1)} %stack.7), calls=%async_computation | async-start | bytes 10485760 | tf_op jit(solution)/shard_map/all_to_all | solution.py:72
  24.9 0.0 copy-start.5
  25.0 0.0 reduce-scatter.3.cloned.1.call-start
  25.0 4.2 fusion.4
  29.2 117.1 %all-to-all-done = bf16[16,320,512]{2,1,0:T(8,128)(2,1)} async-done(((bf16[16,320,512]{2,1,0:T(8,128)(2,1)}), bf16[16,320,512]{2,1,0:T(8,128)(2,1)}, u32[]{:S(2)}, u32[]{:S(2)}) %all-to-all-start) | async-done | bytes 5242912 | tf_op jit(solution)/shard_map/all_to_all | solution.py:72
  146.3 0.0 copy-done.5
  146.3 12.5 %convolution_convert_fusion.1 = bf16[5120,512]{1,0:T(8,128)(2,1)} fusion(f32[384]{0:T(512)S(1)} %add_rsqrt_fusion.1, bf16[1,2,384,5120]{3,2,1,0:T(8,128)(2,1)} %param.10, bf16[5120,512]{1,0:T(8,128)(2,1)} %bitcast.5, bf16[1,2,384,512]{3,2,1,0:T(8,128)(2,1)S(1)} %copy-done.5), kind=kOutput, calls=%fused_computation.15 | convolution fusion | flops 4043112448 | bytes 18747392 | tf_op jit(solution)/shard_map/dot_general | solution.py:86
  158.8 0.0 copy-start
  158.8 0.0 reduce-scatter.3.cloned.1.call-update
  158.8 113.0 %reduce-scatter.3.cloned.1.call-done = bf16[320,512]{1,0:T(8,128)(2,1)} async-done(((bf16[5120,512]{1,0:T(8,128)(2,1)}), bf16[320,512]{1,0:T(8,128)(2,1)}) %reduce-scatter.3.cloned.1.call-update) | async-done | bytes 327696 | tf_op jit(solution)/shard_map/reduce_scatter | solution.py:85
  271.8 0.0 copy-done
  271.8 1.1 fusion.43
  272.9 2.9 stack.8
  275.8 0.0 copy-start.6
  275.8 4.7 all-to-all-start.1
  280.5 0.0 all-gather.5.cloned.1.call-start
  281.2 0.0 copy-done.6
  281.2 0.6 fusion.52
  282.5 0.2 abs_reduce_fusion
  282.6 0.8 divide_convert_fusion
  283.4 0.0 all-gather.5.cloned.1.call-update
  283.4 0.2 reduce-scatter.5.cloned.1.call-start
  283.7 143.9 %all-to-all-done.1 = bf16[16,320,512]{2,1,0:T(8,128)(2,1)} async-done(((bf16[16,320,512]{2,1,0:T(8,128)(2,1)}), bf16[16,320,512]{2,1,0:T(8,128)(2,1)}, u32[]{:S(2)}, u32[]{:S(2)}) %all-to-all-start.1) | async-done | bytes 5242912 | tf_op jit(solution)/shard_map/all_to_all | solution.py:72
  427.5 12.5 %convolution_convert_fusion = bf16[5120,512]{1,0:T(8,128)(2,1)} fusion(f32[384]{0:T(512)S(1)} %add_rsqrt_fusion, bf16[1,2,384,5120]{3,2,1,0:T(8,128)(2,1)} %param.10, bf16[5120,512]{1,0:T(8,128)(2,1)} %bitcast.9, bf16[1,2,384,512]{3,2,1,0:T(8,128)(2,1)S(1)} %copy-done.5), kind=kOutput, calls=%fused_computation.14 | convolution fusion | flops 4043112448 | bytes 18747392 | tf_op jit(solution)/shard_map/dot_general | solution.py:86
  440.0 0.0 copy-start.7
  440.0 0.0 copy-start.2
  440.0 0.0 reduce-scatter.5.cloned.1.call-update
  440.1 34.9 %all-gather.2 = f32[16,20,128]{2,1,0:T(8,128)S(1)} all-gather(f32[1,20,128]{2,1,0:T(8,128)S(1)} %dynamic-slice_bitcast_fusion), channel_id=1, replica_groups=mesh['replica'=16,'fsdp'=16] {'replica'}, dimensions={0}, use_global_device_ids=true | all-gather | bytes 174080 | tf_op jit(solution)/shard_map/all_gather | solution.py:61
  475.0 0.0 copy-done.7
  475.0 0.6 dynamic-slice.1
  476.2 0.3 dynamic-update-slice
  476.5 78.4 %all-reduce = bf16[5120]{0:T(1024)(128)(2,1)S(1)} all-reduce(bf16[5120]{0:T(1024)(128)(2,1)S(1)} %dynamic-update-slice), channel_id=3, replica_groups=mesh['replica'=16,'fsdp'=16] {'replica'}, use_global_device_ids=true, to_apply=%add | all-reduce | flops 5120 | bytes 20480
  554.9 0.1 reshape.86
  555.0 0.0 all-gather.5.cloned.1.call-done
  555.1 1.9 fusion.26
  557.0 0.0 reduce-scatter.5.cloned.1.call-done
  557.0 0.0 copy-done.2
  557.0 1.1 multiply_subtract_fusion
  558.2 0.1 bitcast_dynamic-update-slice_fusion
  558.3 0.0 copy-start.3
  558.3 0.1 multiply_add_fusion
  558.4 0.0 copy-start.1
  558.4 0.0 copy-start.4
  558.4 0.7 copy-done.3
  559.1 0.2 copy-done.1
  559.3 0.0 copy-done.4
  (9 shorter events, 0.1 us)
Async XLA Ops:
  13.9 132.4 %all-to-all-start = ((bf16[16,320,512]{2,1,0:T(8,128)(2,1)}), bf16[16,320,512]{2,1,0:T(8,128)(2,1)}, u32[]{:S(2)}, u32[]{:S(2)}) async-start(bf16[16,320,512]{2,1,0:T(8,128)(2,1)} %stack.7), calls=%async_computation | async-start | bytes 10485760 | tf_op jit(solution)/shard_map/all_to_all | solution.py:72
  24.9 121.4 %copy-start.5 = (bf16[1,2,384,512]{3,2,1,0:T(8,128)(2,1)S(1)}, bf16[1,2,384,512]{3,2,1,0:T(8,128)(2,1)}, u32[]{:S(2)}) copy-start(bf16[1,2,384,512]{3,2,1,0:T(8,128)(2,1)} %param.11) | copy-start | bytes 2359300
  25.0 246.9 %reduce-scatter.3.cloned.1.call-start = ((), (), s32[]{:S(2)}) async-start(), calls=%async_computation.4 | async-start | bytes 5570560 | tf_op jit(solution)/shard_map/reduce_scatter | solution.py:85
  158.8 113.1 %copy-start = (f32[1,320,512]{2,1,0:T(8,128)S(1)}, f32[1,320,512]{2,1,0:T(8,128)}, u32[]{:S(2)}) copy-start(f32[1,320,512]{2,1,0:T(8,128)} %param.7) | copy-start | bytes 1966084
  275.8 5.4 copy-start.6
  275.8 151.8 %all-to-all-start.1 = ((bf16[16,320,512]{2,1,0:T(8,128)(2,1)}), bf16[16,320,512]{2,1,0:T(8,128)(2,1)}, u32[]{:S(2)}, u32[]{:S(2)}) async-start(bf16[16,320,512]{2,1,0:T(8,128)(2,1)} %stack.8), calls=%async_computation.2 | async-start | bytes 10485760 | tf_op jit(solution)/shard_map/all_to_all | solution.py:72
  280.5 274.6 %all-gather.5.cloned.1.call-start = ((), (), s32[]{:S(2)}) async-start(), calls=%async_computation.6 | async-start | bytes 1392640 | tf_op jit(solution)/shard_map/all_gather | solution.py:54
  283.4 273.6 %reduce-scatter.5.cloned.1.call-start = ((), (), s32[]{:S(2)}) async-start(), calls=%async_computation.5 | async-start | bytes 5570560 | tf_op jit(solution)/shard_map/reduce_scatter | solution.py:85
  440.0 35.0 %copy-start.7 = (u32[256]{0:T(256)S(1)}, u32[256]{0:T(256)}, u32[]{:S(2)}) copy-start(u32[256]{0:T(256)} %constant.63) | copy-start | bytes 3076
  440.0 117.0 %copy-start.2 = (bf16[320,512]{1,0:T(8,128)(2,1)S(1)}, bf16[320,512]{1,0:T(8,128)(2,1)}, u32[]{:S(2)}) copy-start(bf16[320,512]{1,0:T(8,128)(2,1)} %reduce-scatter.3.cloned.1.call-done) | copy-start | bytes 983044
  558.3 0.8 copy-start.3
  558.4 1.0 copy-start.1
  558.4 0.9 copy-start.4
Sparse Core Ops, SparseCore 0:
  158.9 112.8 reduce-scatter.2
  440.2 109.0 reduce-scatter.4
Sparse Core Ops, SparseCore 1:
  283.5 92.4 all-gather.4
